TPU v7x, 128 devices: a whole 4x4x4 slice. The times are simulated.
128 devices in a mesh: section: 2 (over x_hi), dp: 16 (over y, x_lo, core), tensor: 4 (over z).
Axes of the slice: x: 4 (x_hi: 2, x_lo: 2; x = x_hi * 2 + x_lo), y: 4, z: 4, core: 2. Of those that a mesh axis runs over, the one named last changes fastest.
Arguments:
- boundary: bfloat16 [2, 2, 16, 576, 1024], P('section', None, 'dp', 'tensor'), may hold values from -6 to 6
- w_qkv: bfloat16 [2, 1024, 3, 1024], P('section', 'dp', None, 'tensor'), may hold values from -0.1875 to 0.1875
- qv_bias: bfloat16 [2, 2, 16, 64], P('section', None, 'tensor', 'dp'), may hold values from -3 to 3
- w_out: bfloat16 [2, 1024, 1024], P('section', 'tensor', 'dp'), may hold values from -1.5 to 1.5
- up_weight: bfloat16 [2, 1024, 4096], P('section', 'dp', 'tensor'), may hold values from -0.1875 to 0.1875
- up_bias: bfloat16 [2, 64, 64], P('section', 'tensor', 'dp'), may hold values from -3 to 3
- down_weight: bfloat16 [2, 4096, 1024], P('section', 'tensor', 'dp'), may hold values from -0.09375 to 0.09375
- norm_bias: bfloat16 [2, 6, 1024], P('section', None, ('dp', 'tensor')), as said below
Outputs:
- ends: float32 [2, 2, 16, 576, 1024], P('section', None, 'dp', 'tensor')
- grad_qkv: float32 [2, 1024, 3, 1024], P('section', 'dp', None, 'tensor')
- grad_qv_bias: float32 [2, 2, 16, 64], P('section', None, 'tensor', 'dp')
- grad_w_out: float32 [2, 1024, 1024], P('section', 'tensor', 'dp')
- grad_up_weight: float32 [2, 1024, 4096], P('section', 'dp', 'tensor')
- grad_up_bias: float32 [2, 64, 64], P('section', 'tensor', 'dp')
- grad_down_weight: float32 [2, 4096, 1024], P('section', 'tensor', 'dp')
- grad_norm_bias: float32 [2, 6, 1024], P('section', None, ('dp', 'tensor'))
Inputs may be any that keep to these rules, and one draw needn't show every extreme that they name: Rows 0 and 3 of norm_bias lie within 0.4 to 1.6, the other rows within -0.9 to 0.9.
All inputs are finite; a program needn't handle non-finite values.
Results may differ from a plain program's by a relative error of at most 0.03.
Values may be sent and summed in bfloat16 or wider, within the bound.
A program may use at most 192 MiB of HBM per device.

v0:
```python
from functools import partial

import jax
import jax.numpy as jnp
from jax import lax
from jax.sharding import Mesh
from jax.sharding import PartitionSpec as P

DP = ("dp_0", "dp_1", "dp_2")
DP_TENSOR = ("dp_0", "dp_1", "dp_2", "tensor")


EPSILON = 1e-06


def laid_out(blocks, dim):
    blocks = jnp.moveaxis(blocks, 0, dim)
    lengths = blocks.shape
    return blocks.reshape(*lengths[:dim], lengths[dim] * lengths[dim + 1], *lengths[dim + 2 :])


def from_everyone(array, axis):
    copies = jnp.broadcast_to(array, (lax.axis_size(axis), *array.shape))
    return lax.all_to_all(copies, axis, split_axis=0, concat_axis=0, tiled=True)


def collect(array, axis, dim):
    return laid_out(from_everyone(array, axis), dim)


def in_blocks(array, dim, peers):
    lengths = array.shape
    blocks = array.reshape(*lengths[:dim], peers, lengths[dim] // peers, *lengths[dim + 1 :])
    return jnp.moveaxis(blocks, dim, 0)


def sum_at_owner(array, axis, dim):
    blocks = in_blocks(array, dim, lax.axis_size(axis))
    arrived = lax.all_to_all(blocks, axis, split_axis=0, concat_axis=0, tiled=True)
    return arrived.sum(axis=0)


def summed_on_arrival(array, axis, dim):
    peers = lax.axis_size(axis)
    blocks = lax.all_to_all(in_blocks(array, dim, peers), axis, 0, 0, tiled=True)
    return jnp.sum(blocks.astype(jnp.float32), axis=0)


def summed_rows(array, axes, dim):
    far, near = axes
    blocks = in_blocks(array, dim, lax.axis_size(far))
    nearer = summed_on_arrival(blocks, near, dim + 1)
    arrived = lax.all_to_all(
        nearer.astype(jnp.bfloat16), far, split_axis=0, concat_axis=0, tiled=True
    )
    return arrived.astype(jnp.float32).sum(axis=0)


def passed_along(value, axis, steps):
    count = lax.axis_size(axis)
    leading, last = (max(0, -steps), min(count, count - steps))
    return lax.ppermute(value, axis, [(source, source + steps) for source in range(leading, last)])


def normalize(tok_rows, gain_row, shift_row):
    centred = tok_rows - jnp.mean(tok_rows, axis=-1, keepdims=True)
    spread = jnp.mean(centred * centred, axis=-1, keepdims=True)
    return centred * lax.rsqrt(spread + EPSILON) * gain_row + shift_row


def fetch_weights(w_qkv, qv_bias, w_out, up_weight, up_bias, down_weight):
    return (
        lax.all_gather(w_qkv[0], DP, axis=0, tiled=True),
        lax.all_gather(qv_bias[0], DP, axis=2, tiled=True),
        lax.all_gather(w_out[0], DP, axis=1, tiled=True),
        lax.all_gather(up_weight[0], DP, axis=0, tiled=True),
        lax.all_gather(up_bias[0], DP, axis=1, tiled=True),
        lax.all_gather(down_weight[0], DP, axis=1, tiled=True),
    )


def spread_rows(values):
    return collect(values, "tensor", 1)


def collect_rows(partial_sum):
    return sum_at_owner(partial_sum, "tensor", 1)


def spread_grads(values):
    return collect(values, "tensor", 1)


def sum_grads(partial_sum):
    return sum_at_owner(partial_sum, "tensor", 1)


def reduce_grads(matrices, vector_grad):
    shards = (
        summed_rows(matrices[0].astype(jnp.bfloat16), (("dp_0", "dp_1"), "dp_2"), 0),
        summed_rows(matrices[1].astype(jnp.bfloat16), (("dp_0", "dp_1"), "dp_2"), 2),
        summed_rows(matrices[2].astype(jnp.bfloat16), (("dp_0", "dp_1"), "dp_2"), 1),
        summed_rows(matrices[3].astype(jnp.bfloat16), (("dp_0", "dp_1"), "dp_2"), 0),
        summed_rows(matrices[4].astype(jnp.bfloat16), (("dp_0", "dp_1"), "dp_2"), 1),
        summed_rows(matrices[5].astype(jnp.bfloat16), (("dp_0", "dp_1"), "dp_2"), 1),
    )
    vector_shard = sum_at_owner(vector_grad, DP_TENSOR, 1)
    return (tuple(shards), vector_shard)


def forward(tok_rows, weights, vectors):
    w_qkv, qv_bias, w_out, up_weight, up_bias, down_weight = weights
    image_count = tok_rows.shape[0]
    heads_here = qv_bias.shape[1]
    head_width = qv_bias.shape[2]
    inner_width = heads_here * head_width
    normed = normalize(tok_rows, vectors[0], vectors[1]).astype(jnp.bfloat16)
    normed_all = spread_rows(normed)
    seq_length = normed_all.shape[1]
    shape_heads = (image_count, seq_length, heads_here, head_width)
    project = jnp.einsum("bld,dke->blke", normed_all, w_qkv, preferred_element_type=jnp.float32)
    query = (project[:, :, 0] + qv_bias[0].reshape(inner_width).astype(jnp.float32)) * 0.125
    query = query.astype(jnp.bfloat16).reshape(shape_heads)
    key_low = project[:, :, 1].astype(jnp.bfloat16).reshape(shape_heads)
    value_low = project[:, :, 2] + qv_bias[1].reshape(inner_width).astype(jnp.float32)
    value_low = value_low.astype(jnp.bfloat16).reshape(shape_heads)
    scores = jnp.einsum("bqhe,bkhe->bhqk", query, key_low, preferred_element_type=jnp.float32)
    row_peak = jnp.max(scores, axis=-1, keepdims=True)
    exponent = jnp.exp(scores - row_peak)
    totals = jnp.sum(exponent, axis=-1, keepdims=True)
    probability = exponent / totals
    logsum = row_peak + jnp.log(totals)
    attended = jnp.einsum(
        "bhqk,bkhe->bqhe",
        probability.astype(jnp.bfloat16),
        value_low,
        preferred_element_type=jnp.float32,
    )
    attended = attended.astype(jnp.bfloat16).reshape(image_count, seq_length, inner_width)
    branch = collect_rows(
        jnp.einsum("ble,ed->bld", attended, w_out, preferred_element_type=jnp.float32)
    )
    middle = tok_rows + branch + vectors[2]
    normed_two = normalize(middle, vectors[3], vectors[4]).astype(jnp.bfloat16)
    normed_two_all = spread_rows(normed_two)
    hidden = jnp.einsum(
        "bld,df->blf", normed_two_all, up_weight, preferred_element_type=jnp.float32
    )
    hidden = hidden + up_bias.reshape(-1).astype(jnp.float32)
    active = jax.nn.gelu(hidden, approximate=False).astype(jnp.bfloat16)
    down_sum = collect_rows(
        jnp.einsum("blf,fd->bld", active, down_weight, preferred_element_type=jnp.float32)
    )
    output = middle + down_sum + vectors[5]
    stored = (
        tok_rows,
        normed_all,
        query,
        key_low,
        value_low,
        logsum,
        attended,
        middle,
        normed_two_all,
        hidden,
        active,
    )
    return (output, stored)


def backward(grad_output, stored, weights, vectors):
    w_qkv, qv_bias, w_out, up_weight, up_bias, down_weight = weights
    (
        tok_rows,
        normed_all,
        query,
        key_low,
        value_low,
        logsum,
        attended,
        middle,
        normed_two_all,
        hidden,
        active,
    ) = stored
    image_count, seq_length, heads_here, head_width = query.shape
    inner_width = heads_here * head_width
    grad_shift_end = jnp.sum(grad_output, axis=(0, 1))
    grad_all = spread_grads(grad_output.astype(jnp.bfloat16))
    grad_down_w = jnp.einsum("blf,bld->fd", active, grad_all, preferred_element_type=jnp.float32)
    grad_active = jnp.einsum(
        "bld,fd->blf", grad_all, down_weight, preferred_element_type=jnp.float32
    )
    gelu_pull = jax.vjp(partial(jax.nn.gelu, approximate=False), hidden)[1]
    grad_hidden = gelu_pull(grad_active)[0].astype(jnp.bfloat16)
    grad_up_bias = jnp.sum(grad_hidden, axis=(0, 1), dtype=jnp.float32).reshape(up_bias.shape)
    grad_up_w = jnp.einsum(
        "bld,blf->df", normed_two_all, grad_hidden, preferred_element_type=jnp.float32
    )
    grad_normed_two = sum_grads(
        jnp.einsum("blf,df->bld", grad_hidden, up_weight, preferred_element_type=jnp.float32)
    )
    second_pull = jax.vjp(normalize, middle, vectors[3], vectors[4])[1]
    grad_mid_norm, grad_gain_two, grad_shift_two = second_pull(grad_normed_two)
    grad_middle = grad_output + grad_mid_norm
    grad_bias_out = jnp.sum(grad_middle, axis=(0, 1))
    grad_mid_all = spread_grads(grad_middle.astype(jnp.bfloat16))
    grad_out_w = jnp.einsum(
        "ble,bld->ed", attended, grad_mid_all, preferred_element_type=jnp.float32
    )
    grad_attended = jnp.einsum(
        "bld,ed->ble", grad_mid_all, w_out, preferred_element_type=jnp.float32
    )
    grad_attended = grad_attended.astype(jnp.bfloat16).reshape(query.shape)
    scores = jnp.einsum("bqhe,bkhe->bhqk", query, key_low, preferred_element_type=jnp.float32)
    probability = jnp.exp(scores - logsum)
    grad_values = jnp.einsum(
        "bhqk,bqhe->bkhe",
        probability.astype(jnp.bfloat16),
        grad_attended,
        preferred_element_type=jnp.float32,
    ).astype(jnp.bfloat16)
    grad_probs = jnp.einsum(
        "bqhe,bkhe->bhqk", grad_attended, value_low, preferred_element_type=jnp.float32
    )
    grad_scores = probability * (
        grad_probs - jnp.sum(grad_probs * probability, axis=-1, keepdims=True)
    )
    grad_scores = grad_scores.astype(jnp.bfloat16)
    grad_query = (
        jnp.einsum(
            "bhqk,bkhe->bqhe", grad_scores, key_low, preferred_element_type=jnp.float32
        ).astype(jnp.bfloat16)
        * 0.125
    )
    grad_keys = jnp.einsum(
        "bhqk,bqhe->bkhe", grad_scores, query, preferred_element_type=jnp.float32
    ).astype(jnp.bfloat16)
    flat_shape = (image_count, seq_length, inner_width)
    grad_project = jnp.stack(
        [
            grad_query.reshape(flat_shape),
            grad_keys.reshape(flat_shape),
            grad_values.reshape(flat_shape),
        ],
        axis=2,
    )
    grad_qkv_w = jnp.einsum(
        "bld,blke->dke", normed_all, grad_project, preferred_element_type=jnp.float32
    )
    grad_qv = jnp.stack(
        [
            jnp.sum(grad_query, axis=(0, 1), dtype=jnp.float32),
            jnp.sum(grad_values, axis=(0, 1), dtype=jnp.float32),
        ]
    )
    grad_normed = sum_grads(
        jnp.einsum("blke,dke->bld", grad_project, w_qkv, preferred_element_type=jnp.float32)
    )
    first_pull = jax.vjp(normalize, tok_rows, vectors[0], vectors[1])[1]
    grad_rows_norm, grad_gain_one, grad_shift_one = first_pull(grad_normed)
    grad_rows = grad_middle + grad_rows_norm
    grad_vectors = jnp.stack(
        [
            grad_gain_one,
            grad_shift_one,
            grad_bias_out,
            grad_gain_two,
            grad_shift_two,
            grad_shift_end,
        ]
    )
    matrices = (grad_qkv_w, grad_qv, grad_out_w, grad_up_w, grad_up_bias, grad_down_w)
    return (grad_rows, matrices, grad_vectors)


def body(boundary, w_qkv, qv_bias, w_out, up_weight, up_bias, down_weight, norm_bias):
    micro_count = boundary.shape[1]
    first_section = lax.axis_index("section") == 0
    vectors = collect(norm_bias[0], DP_TENSOR, 1).astype(jnp.float32)
    incoming = jnp.zeros(boundary.shape[2:], jnp.float32)
    saved_list = []
    finals = []
    for tick_index in range(micro_count + 1):
        weights = fetch_weights(w_qkv, qv_bias, w_out, up_weight, up_bias, down_weight)
        own_input = boundary[0, min(tick_index, micro_count - 1)].astype(jnp.float32)
        tok_rows = jnp.where(first_section, own_input, incoming)
        output, stored = forward(tok_rows, weights, vectors)
        saved_list.append(stored)
        if tick_index >= 1:
            finals.append(output)
        if tick_index < micro_count:
            incoming = passed_along(output.astype(jnp.bfloat16), "section", 1).astype(jnp.float32)
    arriving = jnp.zeros(boundary.shape[2:], jnp.float32)
    input_grads = []
    total_mats = None
    total_vectors = None
    for tick_index in range(micro_count + 1):
        weights = fetch_weights(w_qkv, qv_bias, w_out, up_weight, up_bias, down_weight)
        cotangent = boundary[0, min(tick_index, micro_count - 1)].astype(jnp.float32)
        grad_output = jnp.where(first_section, arriving, cotangent)
        earlier_saved = saved_list[max(tick_index - 1, 0)]
        later_saved = saved_list[min(tick_index + 1, micro_count)]
        stored = jax.tree.map(
            lambda earlier, later: jnp.where(first_section, earlier, later),
            earlier_saved,
            later_saved,
        )
        valid_mask = jnp.where(first_section, tick_index >= 1, tick_index < micro_count).astype(
            jnp.float32
        )
        grad_rows, matrices, grad_vectors = backward(grad_output, stored, weights, vectors)
        matrices = tuple((matrix * valid_mask for matrix in matrices))
        grad_vectors = grad_vectors * valid_mask
        matrices, grad_vectors = reduce_grads(matrices, grad_vectors)
        if total_mats is None:
            total_mats = matrices
            total_vectors = grad_vectors
        else:
            total_mats = tuple((running + update for running, update in zip(total_mats, matrices)))
            total_vectors = total_vectors + grad_vectors
        if tick_index >= 1:
            input_grads.append(grad_rows)
        if tick_index < micro_count:
            arriving = passed_along(grad_rows.astype(jnp.bfloat16), "section", -1).astype(
                jnp.float32
            )
    ends = jnp.where(first_section, jnp.stack(input_grads), jnp.stack(finals))[None]
    return (
        ends,
        total_mats[0][None],
        total_mats[1][None],
        total_mats[2][None],
        total_mats[3][None],
        total_mats[4][None],
        total_mats[5][None],
        total_vectors[None],
    )


def solution(mesh):
    torus = Mesh(
        mesh.devices.reshape(mesh.shape["section"], 4, 2, 2, mesh.shape["tensor"]),
        ("section", "dp_0", "dp_1", "dp_2", "tensor"),
    )
    in_specs = (
        P("section", None, DP, "tensor", None),
        P("section", DP, None, "tensor"),
        P("section", None, "tensor", DP),
        P("section", "tensor", DP),
        P("section", DP, "tensor"),
        P("section", "tensor", DP),
        P("section", "tensor", DP),
        P("section", None, DP_TENSOR),
    )
    out_specs = (
        P("section", None, DP, "tensor", None),
        P("section", DP, None, "tensor"),
        P("section", None, "tensor", DP),
        P("section", "tensor", DP),
        P("section", DP, "tensor"),
        P("section", "tensor", DP),
        P("section", "tensor", DP),
        P("section", None, DP_TENSOR),
    )
    return jax.shard_map(body, mesh=torus, in_specs=in_specs, out_specs=out_specs, check_vma=False)
```

profile of v0, /device:TPU:1, one launch (start us, length us, event | category | flops | bytes accessed | tf_op | source)
XLA Modules:
  0.0 1263.6 jit_solution(16568100446278286984)
XLA Ops:
  9.3 10.9 all-to-all-start
  35.0 17.9 %all-gather.1 = bf16[1,2,4,64]{2,1,0,3:T(2,128)(2,1)S(1)} all-gather(bf16[1,2,4,4]{2,1,0,3:T(2,128)(2,1)S(1)} %copy.652), channel_id=3, replica_groups=mesh['section'=2,'dp_0'=4,'dp_1'=2,'dp_2'=2,'tensor'=4] {'dp_0','dp_1','..., dimensions={3}, use_global_device_ids=true | all-gather | bytes 1088 | tf_op jit(solution)/shard_map/all_gather | solution.py:74
  53.0 19.6 %all-gather.2 = bf16[1,256,1024]{1,2,0:T(8,128)(2,1)S(1)} all-gather(bf16[1,256,64]{1,2,0:T(8,128)(2,1)S(1)} %copy-done.131), channel_id=4, replica_groups=mesh['section'=2,'dp_0'=4,'dp_1'=2,'dp_2'=2,'tensor'=4] {'dp_0','dp_1','..., dimensions={2}, use_global_device_ids=true | all-gather | bytes 557056 | tf_op jit(solution)/shard_map/all_gather | solution.py:75
  93.2 28.4 %all-to-all-done.2 = f32[4,1,144,1024]{3,2,1,0:T(8,128)} async-done(((f32[4,1,144,1024]{3,2,1,0:T(8,128)}), f32[4,1,144,1024]{3,2,1,0:T(8,128)}, u32[]{:S(2)}, u32[]{:S(2)}) %all-to-all-start.2) | async-done | bytes 2359328 | tf_op jit(solution)/shard_map/all_to_all | solution.py:39
  129.6 19.9 %all-gather.4 = bf16[1,16,64]{1,0,2:T(2,128)(2,1)S(1)} all-gather(bf16[1,16,4]{1,0,2:T(2,128)(2,1)S(1)} %copy.661), channel_id=6, replica_groups=mesh['section'=2,'dp_0'=4,'dp_1'=2,'dp_2'=2,'tensor'=4] {'dp_0','dp_1','..., dimensions={2}, use_global_device_ids=true | all-gather | bytes 2176 | tf_op jit(solution)/shard_map/all_gather | solution.py:77
  168.1 29.3 %all-to-all-done.4 = f32[4,1,144,1024]{3,2,1,0:T(8,128)} async-done(((f32[4,1,144,1024]{3,2,1,0:T(8,128)}), f32[4,1,144,1024]{3,2,1,0:T(8,128)}, u32[]{:S(2)}, u32[]{:S(2)}) %all-to-all-start.4) | async-done | bytes 2359328 | tf_op jit(solution)/shard_map/all_to_all | solution.py:39
  209.6 16.9 %all_to_all.320 = bf16[4,1,144,1024]{3,2,1,0:T(8,128)(2,1)S(1)} all-to-all(bf16[4,1,144,1024]{3,2,1,0:T(8,128)(2,1)S(1)} %broadcast_in_dim.53), channel_id=1, replica_groups=mesh['section'=2,'dp_0'=4,'dp_1'=2,'dp_2'=2,'tensor'=4] {'tensor'}, dimensions={0} | all-to-all | bytes 2359296 | tf_op jit(solution)/shard_map/all_to_all | solution.py:24
  243.9 29.6 %all_to_all.321 = f32[4,1,144,1024]{3,2,1,0:T(8,128)} all-to-all(f32[4,1,144,1024]{3,2,1,0:T(8,128)S(1)} %convolution_bitcast_fusion.4), channel_id=1, replica_groups=mesh['section'=2,'dp_0'=4,'dp_1'=2,'dp_2'=2,'tensor'=4] {'tensor'}, dimensions={0} | all-to-all | bytes 4718592 | tf_op jit(solution)/shard_map/all_to_all | solution.py:39
  279.1 15.3 %all_to_all.322 = bf16[4,1,144,1024]{3,2,1,0:T(8,128)(2,1)} all-to-all(bf16[4,1,144,1024]{3,2,1,0:T(8,128)(2,1)S(1)} %broadcast_in_dim.54), channel_id=1, replica_groups=mesh['section'=2,'dp_0'=4,'dp_1'=2,'dp_2'=2,'tensor'=4] {'tensor'}, dimensions={0} | all-to-all | bytes 2359296 | tf_op jit(solution)/shard_map/all_to_all | solution.py:24
  310.9 9.7 convert_reduce_fusion.1
  333.9 17.6 %all-to-all-done.9 = f32[4,1,144,1024]{3,2,1,0:T(8,128)} async-done(((f32[4,1,144,1024]{3,2,1,0:T(8,128)}), f32[4,1,144,1024]{3,2,1,0:T(8,128)}, u32[]{:S(2)}, u32[]{:S(2)}) %all-to-all-start.9) | async-done | bytes 2359328 | tf_op jit(solution)/shard_map/all_to_all | solution.py:39
  359.1 18.0 %all-to-all-done.12 = f32[4,1,144,1024]{3,2,1,0:T(8,128)} async-done(((f32[4,1,144,1024]{3,2,1,0:T(8,128)}), f32[4,1,144,1024]{3,2,1,0:T(8,128)}, u32[]{:S(2)}, u32[]{:S(2)}) %all-to-all-start.12) | async-done | bytes 2359328 | tf_op jit(solution)/shard_map/all_to_all | solution.py:39
  436.1 17.7 %all-to-all-done.11 = f32[4,1,144,1024]{3,2,1,0:T(8,128)} async-done(((f32[4,1,144,1024]{3,2,1,0:T(8,128)}), f32[4,1,144,1024]{3,2,1,0:T(8,128)}, u32[]{:S(2)}, u32[]{:S(2)}) %all-to-all-start.11) | async-done | bytes 2359328 | tf_op jit(solution)/shard_map/all_to_all | solution.py:39
  486.5 16.5 %all-to-all-start.49 = ((bf16[2,2,256]{2,1,0:T(2,128)(2,1)}), bf16[2,2,256]{2,1,0:T(2,128)(2,1)S(1)}, u32[]{:S(2)}, u32[]{:S(2)}) async-start(bf16[2,2,256]{2,1,0:T(2,128)(2,1)} %reshape.3271), calls=%async_computation.49 | async-start | bytes 4096 | tf_op jit(solution)/shard_map/all_to_all | solution.py:45
  549.5 18.3 %all-to-all-done.14 = f32[4,1,144,1024]{3,2,1,0:T(8,128)} async-done(((f32[4,1,144,1024]{3,2,1,0:T(8,128)}), f32[4,1,144,1024]{3,2,1,0:T(8,128)}, u32[]{:S(2)}, u32[]{:S(2)}) %all-to-all-start.14) | async-done | bytes 2359328 | tf_op jit(solution)/shard_map/all_to_all | solution.py:39
  627.6 9.9 fusion.295
  641.4 13.7 %all-to-all-done.24 = f32[4,1,144,1024]{3,2,1,0:T(8,128)} async-done(((f32[4,1,144,1024]{3,2,1,0:T(8,128)}), f32[4,1,144,1024]{3,2,1,0:T(8,128)}, u32[]{:S(2)}, u32[]{:S(2)}) %all-to-all-start.24) | async-done | bytes 2359328 | tf_op jit(solution)/shard_map/all_to_all | solution.py:39
  674.9 11.5 all-to-all-done.17
  841.2 16.7 %all-to-all-done.19 = f32[4,1,144,1024]{3,2,1,0:T(8,128)} async-done(((f32[4,1,144,1024]{3,2,1,0:T(8,128)}), f32[4,1,144,1024]{3,2,1,0:T(8,128)}, u32[]{:S(2)}, u32[]{:S(2)}) %all-to-all-start.19) | async-done | bytes 2359328 | tf_op jit(solution)/shard_map/all_to_all | solution.py:39
  914.4 10.3 convert_reduce_fusion
  928.7 9.8 all_to_all.329
  991.5 12.2 all-to-all-done.46
  1216.7 12.4 all-to-all-done.23
  1235.6 10.0 all-to-all-start.63
  (871 shorter events, 854.4 us)
Async XLA Ops:
  7.2 65.5 %all-gather.10.cloned.1.call-start = ((), (), s32[]{:S(2)}) async-start(), calls=%async_computation.64 | async-start | bytes 1671168 | tf_op jit(solution)/shard_map/all_gather | solution.py:73
  30.6 42.1 %all-to-all-start.1 = ((bf16[4,1,144,1024]{3,2,1,0:T(8,128)(2,1)}), bf16[4,1,144,1024]{3,2,1,0:T(8,128)(2,1)S(1)}, u32[]{:S(2)}, u32[]{:S(2)}) async-start(bf16[4,1,144,1024]{3,2,1,0:T(8,128)(2,1)} %broadcast_in_dim.51), calls=%async_computation.1 | async-start | bytes 2359296 | tf_op jit(solution)/shard_map/all_to_all | solution.py:24
  34.1 115.5 %all-gather.12.cloned.1.call-start = ((), (), s32[]{:S(2)}) async-start(), calls=%async_computation.65 | async-start | bytes 2228224 | tf_op jit(solution)/shard_map/all_gather | solution.py:76
  87.1 34.5 %all-to-all-start.2 = ((f32[4,1,144,1024]{3,2,1,0:T(8,128)}), f32[4,1,144,1024]{3,2,1,0:T(8,128)}, u32[]{:S(2)}, u32[]{:S(2)}) async-start(f32[4,1,144,1024]{3,2,1,0:T(8,128)} %convolution_bitcast_fusion.5), calls=%async_computation.2 | async-start | bytes 4718592 | tf_op jit(solution)/shard_map/all_to_all | solution.py:39
  92.2 66.5 %all-gather.14.cloned.1.call-start = ((), (), s32[]{:S(2)}) async-start(), calls=%async_computation.66 | async-start | bytes 2228224 | tf_op jit(solution)/shard_map/all_gather | solution.py:78
  125.3 24.3 %all-to-all-start.3 = ((bf16[4,1,144,1024]{3,2,1,0:T(8,128)(2,1)}), bf16[4,1,144,1024]{3,2,1,0:T(8,128)(2,1)}, u32[]{:S(2)}, u32[]{:S(2)}) async-start(bf16[4,1,144,1024]{3,2,1,0:T(8,128)(2,1)} %broadcast_in_dim.52), calls=%async_computation.3 | async-start | bytes 2359296 | tf_op jit(solution)/shard_map/all_to_all | solution.py:24
  163.5 33.9 %all-to-all-start.4 = ((f32[4,1,144,1024]{3,2,1,0:T(8,128)}), f32[4,1,144,1024]{3,2,1,0:T(8,128)}, u32[]{:S(2)}, u32[]{:S(2)}) async-start(f32[4,1,144,1024]{3,2,1,0:T(8,128)} %fusion.117), calls=%async_computation.4 | async-start | bytes 4718592 | tf_op jit(solution)/shard_map/all_to_all | solution.py:39
  324.5 27.0 %all-to-all-start.9 = ((f32[4,1,144,1024]{3,2,1,0:T(8,128)}), f32[4,1,144,1024]{3,2,1,0:T(8,128)}, u32[]{:S(2)}, u32[]{:S(2)}) async-start(f32[4,1,144,1024]{3,2,1,0:T(8,128)} %fusion.108), calls=%async_computation.9 | async-start | bytes 4718592 | tf_op jit(solution)/shard_map/all_to_all | solution.py:39
  351.5 25.7 %all-to-all-start.12 = ((f32[4,1,144,1024]{3,2,1,0:T(8,128)}), f32[4,1,144,1024]{3,2,1,0:T(8,128)}, u32[]{:S(2)}, u32[]{:S(2)}) async-start(f32[4,1,144,1024]{3,2,1,0:T(8,128)} %fusion.120), calls=%async_computation.12 | async-start | bytes 4718592 | tf_op jit(solution)/shard_map/all_to_all | solution.py:39
  431.2 22.6 %all-to-all-start.11 = ((f32[4,1,144,1024]{3,2,1,0:T(8,128)}), f32[4,1,144,1024]{3,2,1,0:T(8,128)}, u32[]{:S(2)}, u32[]{:S(2)}) async-start(f32[4,1,144,1024]{3,2,1,0:T(8,128)} %convolution_bitcast_fusion.2), calls=%async_computation.11 | async-start | bytes 4718592 | tf_op jit(solution)/shard_map/all_to_all | solution.py:39
  486.5 35.6 %all-to-all-start.49 = ((bf16[2,2,256]{2,1,0:T(2,128)(2,1)}), bf16[2,2,256]{2,1,0:T(2,128)(2,1)S(1)}, u32[]{:S(2)}, u32[]{:S(2)}) async-start(bf16[2,2,256]{2,1,0:T(2,128)(2,1)} %reshape.3271), calls=%async_computation.49 | async-start | bytes 4096 | tf_op jit(solution)/shard_map/all_to_all | solution.py:45
  534.0 33.8 %all-to-all-start.14 = ((f32[4,1,144,1024]{3,2,1,0:T(8,128)}), f32[4,1,144,1024]{3,2,1,0:T(8,128)}, u32[]{:S(2)}, u32[]{:S(2)}) async-start(f32[4,1,144,1024]{3,2,1,0:T(8,128)} %convolution_bitcast_fusion.3), calls=%async_computation.14 | async-start | bytes 4718592 | tf_op jit(solution)/shard_map/all_to_all | solution.py:39
  581.1 21.5 %all-to-all-start.15 = ((bf16[4,1,144,1024]{3,2,1,0:T(8,128)(2,1)}), bf16[4,1,144,1024]{3,2,1,0:T(8,128)(2,1)}, u32[]{:S(2)}, u32[]{:S(2)}) async-start(bf16[4,1,144,1024]{3,2,1,0:T(8,128)(2,1)} %broadcast_in_dim.62), calls=%async_computation.15 | async-start | bytes 2359296 | tf_op jit(solution)/shard_map/all_to_all | solution.py:24
  603.8 19.3 %all-to-all-start.16 = ((bf16[4,1,144,1024]{3,2,1,0:T(8,128)(2,1)}), bf16[4,1,144,1024]{3,2,1,0:T(8,128)(2,1)S(1)}, u32[]{:S(2)}, u32[]{:S(2)}) async-start(bf16[4,1,144,1024]{3,2,1,0:T(8,128)(2,1)} %broadcast_in_dim.63), calls=%async_computation.16 | async-start | bytes 2359296 | tf_op jit(solution)/shard_map/all_to_all | solution.py:24
  623.1 32.1 %all-to-all-start.24 = ((f32[4,1,144,1024]{3,2,1,0:T(8,128)}), f32[4,1,144,1024]{3,2,1,0:T(8,128)}, u32[]{:S(2)}, u32[]{:S(2)}) async-start(f32[4,1,144,1024]{3,2,1,0:T(8,128)} %fusion.123), calls=%async_computation.24 | async-start | bytes 4718592 | tf_op jit(solution)/shard_map/all_to_all | solution.py:39
  655.1 31.3 %all-to-all-start.17 = ((f32[4,1,144,1024]{3,2,1,0:T(8,128)}), f32[4,1,144,1024]{3,2,1,0:T(8,128)}, u32[]{:S(2)}, u32[]{:S(2)}) async-start(f32[4,1,144,1024]{3,2,1,0:T(8,128)} %fusion.111), calls=%async_computation.17 | async-start | bytes 4718592 | tf_op jit(solution)/shard_map/all_to_all | solution.py:39
  699.9 20.1 %all-to-all-start.18 = ((bf16[4,1,144,1024]{3,2,1,0:T(8,128)(2,1)}), bf16[4,1,144,1024]{3,2,1,0:T(8,128)(2,1)S(1)}, u32[]{:S(2)}, u32[]{:S(2)}) async-start(bf16[4,1,144,1024]{3,2,1,0:T(8,128)(2,1)} %broadcast_in_dim.66), calls=%async_computation.18 | async-start | bytes 2359296 | tf_op jit(solution)/shard_map/all_to_all | solution.py:24
  826.0 31.8 %all-to-all-start.19 = ((f32[4,1,144,1024]{3,2,1,0:T(8,128)}), f32[4,1,144,1024]{3,2,1,0:T(8,128)}, u32[]{:S(2)}, u32[]{:S(2)}) async-start(f32[4,1,144,1024]{3,2,1,0:T(8,128)} %convolution_bitcast_fusion.1), calls=%async_computation.19 | async-start | bytes 4718592 | tf_op jit(solution)/shard_map/all_to_all | solution.py:39
  942.8 40.4 %all-to-all-start.21 = ((f32[4,1,144,1024]{3,2,1,0:T(8,128)}), f32[4,1,144,1024]{3,2,1,0:T(8,128)S(1)}, u32[]{:S(2)}, u32[]{:S(2)}) async-start(f32[4,1,144,1024]{3,2,1,0:T(8,128)} %fusion.114), calls=%async_computation.21 | async-start | bytes 4718592 | tf_op jit(solution)/shard_map/all_to_all | solution.py:39
  983.2 20.5 %all-to-all-start.46 = ((bf16[8,64,1024]{2,1,0:T(8,128)(2,1)}), bf16[8,64,1024]{2,1,0:T(8,128)(2,1)}, u32[]{:S(2)}, u32[]{:S(2)}) async-start(bf16[8,64,1024]{2,1,0:T(8,128)(2,1)} %reduce_sum.1349), calls=%async_computation.46 | async-start | bytes 2097152 | tf_op jit(solution)/shard_map/all_to_all | solution.py:53
  1048.7 20.3 %all-to-all-start.22 = ((bf16[4,1,144,1024]{3,2,1,0:T(8,128)(2,1)}), bf16[4,1,144,1024]{3,2,1,0:T(8,128)(2,1)}, u32[]{:S(2)}, u32[]{:S(2)}) async-start(bf16[4,1,144,1024]{3,2,1,0:T(8,128)(2,1)} %broadcast_in_dim.72), calls=%async_computation.22 | async-start | bytes 2359296 | tf_op jit(solution)/shard_map/all_to_all | solution.py:24
  1133.2 22.5 %all-to-all-start.48 = ((bf16[8,64,1024]{2,1,0:T(8,128)(2,1)}), bf16[8,64,1024]{2,1,0:T(8,128)(2,1)}, u32[]{:S(2)}, u32[]{:S(2)}) async-start(bf16[8,64,1024]{2,1,0:T(8,128)(2,1)} %reduce_sum.1351), calls=%async_computation.48 | async-start | bytes 2097152 | tf_op jit(solution)/shard_map/all_to_all | solution.py:53
  1200.5 28.6 %all-to-all-start.23 = ((f32[4,1,144,1024]{3,2,1,0:T(8,128)}), f32[4,1,144,1024]{3,2,1,0:T(8,128)S(1)}, u32[]{:S(2)}, u32[]{:S(2)}) async-start(f32[4,1,144,1024]{3,2,1,0:T(8,128)} %convolution_bitcast_fusion), calls=%async_computation.23 | async-start | bytes 4718592 | tf_op jit(solution)/shard_map/all_to_all | solution.py:39
  1235.6 19.4 %all-to-all-start.63 = ((f32[64,6,16]{2,1,0:T(8,128)}), f32[64,6,16]{2,1,0:T(8,128)}, u32[]{:S(2)}, u32[]{:S(2)}) async-start(f32[64,6,16]{2,1,0:T(8,128)} %copy.757), calls=%async_computation.63 | async-start | bytes 524288 | tf_op jit(solution)/shard_map/all_to_all | solution.py:39
  (221 other events, 5095.7 us)
Sparse Core Ops, SparseCore 0:
  9.7 36.8 all-gather.9
  48.2 34.4 all-gather.11
  94.7 34.0 all-gather.13
where the time goes:
time: 1280 us; the launch traced here: 1260 us
  waiting for transfers between devices  328 us (26%)
  starting transfers between devices  243 us (19%)
  blocking collectives  215 us (17%)
  matrix products  201 us (16%)
  other arithmetic  143 us (11%)
  local copies, waits for them, and re-layouts  116 us (9%)
  between operations  17 us (1%)
    all_to_all x14, waiting for transfers between devices, sum_at_owner(): lax.all_to_all(blocks, axis, split_axis=0, concat_axis=0, tiled=True)  200 us
    all_to_all x15, blocking collectives, summed_on_arrival(): lax.all_to_all(in_blocks(array, dim, peers), axis, 0, 0, tiled=True)  95.8 us
    all_to_all x14, starting transfers between devices, sum_at_owner(): lax.all_to_all(blocks, axis, split_axis=0, concat_axis=0, tiled=True)  75.1 us
    all_to_all x18, starting transfers between devices, summed_rows(): lax.all_to_all(nearer.astype(jnp.bfloat16), far, split_axis=0, concat_axi...  74 us
    all_to_all x18, waiting for transfers between devices, summed_rows(): lax.all_to_all(nearer.astype(jnp.bfloat16), far, split_axis=0, concat_axi...  62.3 us
    all_to_all x11, starting transfers between devices, from_everyone(): return lax.all_to_all(copies, axis, split_axis=0, concat_axis=0, tiled=True)  52.6 us
    all_to_all x11, waiting for transfers between devices, from_everyone(): return lax.all_to_all(copies, axis, split_axis=0, concat_axis=0, tiled=True)  40.9 us
    all_to_all x2, blocking collectives, from_everyone(): return lax.all_to_all(copies, axis, split_axis=0, concat_axis=0, tiled=True)  32.2 us
  transfers between devices with their start and end apart: 53, of which 38 were waited for; matrix products, arithmetic and copies ran while one was open for 28% of the time, Pallas kernels for 0%

commit v1 on v0

v1 whole, which is shorter than its diff:
```python
from functools import partial
from types import SimpleNamespace
from typing import Any, NamedTuple

import jax
import jax.numpy as jnp
from jax import lax
from jax.experimental import pallas as pl
from jax.experimental.pallas import tpu as pltpu
from jax.sharding import Mesh
from jax.sharding import PartitionSpec as P

AXES = SECTION, DP_Y, DP_X, CORE, TENSOR = ("section", "dp_0", "dp_1", "dp_2", "tensor")
DP = (DP_Y, DP_X, CORE)
DP_TENSOR = (DP_Y, DP_X, CORE, TENSOR)
MESH = pl.DeviceIdType.MESH
BF, F32 = jnp.bfloat16, jnp.float32

X, Y, Z = "x", "y", "z"
SMALL, GRADS, TOTAL, PART, VEC, READY = "small", "grads", "total", "part", "vec", "ready"
EPSILON = 1e-06
T = 576
D = 1024
TILE = 144
N_TILES = T // TILE
SIZE = {Y: 4, X: 2, Z: 4}
NAME = {Y: DP_Y, X: DP_X, Z: TENSOR}

ORDERS = ((X, Y, Z), (X, Z, Y), (Y, Z, X), (Z, Y, X))
ROWS = ((48, 48, 16, 16), (48, 32, 32, 16), (32, 48, 16, 32))
MAX_ROWS = (48, 48, 32, 32)

NT = (((1,), (1,)), ((), ()))
TN = (((0,), (0,)), ((), ()))


def dot(a, b):
    return jnp.dot(a, b, preferred_element_type=F32)


def dot_nt(a, b):
    return lax.dot_general(a, b, NT, preferred_element_type=F32)


def dot_tn(a, b):
    return lax.dot_general(a, b, TN, preferred_element_type=F32)


class Step(NamedTuple):
    waits: list
    cost: float = 0.0
    sends: list = ()
    op: Any = None
    where: Any = None


RATE, LATENCY = 43500.0, 1.0


def in_order(chains, rate=RATE, latency=LATENCY):
    link_free = {}
    arrives = {}
    clock = 0.0
    place = [0] * len(chains)
    order = []
    while True:
        best = None
        for index, chain in enumerate(chains):
            if place[index] == len(chain):
                continue
            step = chain[place[index]]
            if any(task not in arrives for task in step.waits):
                continue
            ready = max([arrives[task] for task in step.waits], default=0.0)
            ready = max(ready, clock)
            if best is None or ready < best[0] - 1e-9:
                best = (ready, index)
        if best is None:
            assert all(p == len(c) for p, c in zip(place, chains))
            return order
        ready, index = best
        step = chains[index][place[index]]
        place[index] += 1
        clock = ready + step.cost
        for task, link, size in step.sends:
            if link is None:
                arrives[task] = clock
                continue
            begin = max(clock, link_free.get(link, 0.0))
            fast = 6.0 if link == CORE else 1.0
            link_free[link] = begin + size / rate / fast
            arrives[task] = link_free[link] + latency
            clock += 0.05
        order.append(step)


def note(*key):
    return (key, None, 0)


EDGE_TASKS = [((READY, 2), READY, 295000)]
CROSS_TASK = ((READY, 3), CORE, 590000)


def bytes_of(done, axis_fixed, rows, columns):
    blocks = 1
    for axis in done:
        blocks *= SIZE[axis]
    return blocks * rows * columns * 2


def gather_chain(group, order):
    rows = 8 if group == SMALL else ROWS[group][order]
    steps, waits, done = [], [], []
    for axis in ORDERS[order]:
        full = bytes_of(done, axis, rows, 512)
        key = (group, order, axis)
        if axis == X:
            steps.append(Step(waits, 0.0, [(key + ("s",), X, full)]))
            waits = [key + ("s",)]
        else:
            steps.append(Step(waits, 0.0, [(key + ("s+",), axis + "+", full), (key + ("s-",), axis + "-", full)]))
            steps.append(Step([key + ("s+",)], 0.0, [(key + ("f+",), axis + "+", full / 2)]))
            steps.append(Step([key + ("s-",)], 0.0, [(key + ("f-",), axis + "-", full / 2)]))
            waits = [key + ("f+",), key + ("f-",)]
        done.append(axis)
    steps.append(Step(waits, 0.0, [note(group, order)]))
    return steps


def reduce_chain(group, order, add):
    rows = ROWS[group][order]
    steps, end, cost = [], None, 0.0
    waits = [(GRADS, group)]
    left = list(ORDERS[order])
    per = 2e-6

    def step(waits, cost, op, sends):
        run = None if op is None else (lambda: add(group, order, op))
        steps.append(Step(waits, cost, sends, run))

    while left:
        axis = left.pop()
        full = bytes_of(left, axis, rows, 512)
        key = (GRADS, group, order, axis)
        if axis == X:
            step(waits, cost, end, [(key + ("s",), X, full)])
            waits = [key + ("s",)]
        else:
            step(waits, cost, end, [(key + ("h+",), axis + "+", full / 2), (key + ("h-",), axis + "-", full / 2)])
            step([key + ("h+",)], 0.2 + full / 4 * per, (axis, "h+"), [(key + ("s+",), axis + "+", full)])
            step([key + ("h-",)], 0.2 + full / 4 * per, (axis, "h-"), [(key + ("s-",), axis + "-", full)])
            waits = [key + ("s+",), key + ("s-",)]
        end = (axis, "end")
        cost = 0.2 + full * per
    step(waits, cost, end, [note(TOTAL, group, order)])
    return steps


GATHER_TASKS = {}
REDUCE_TASKS = {}
for _axes in ORDERS:
    for _axis in _axes:
        for _kind in ("s",) if _axis == X else ("s+", "s-", "f+", "f-"):
            GATHER_TASKS.setdefault((_axes, _axis, _kind), len(GATHER_TASKS))
        for _kind in ("s",) if _axis == X else ("s+", "s-", "h+", "h-"):
            REDUCE_TASKS.setdefault((_axes, _axis, _kind), len(REDUCE_TASKS))
N_TASKS = len(GATHER_TASKS)
N_SMALL = 9


def landing_shapes():
    shapes = {}
    for order, axes in enumerate(ORDERS):
        left = list(axes)
        while left:
            axis = left.pop()
            lead = tuple(SIZE[a] for a in (Z, Y, X) if a in left)
            for kind in ("s",) if axis == X else ("s+", "s-", "h+", "h-"):
                columns = 256 if kind[0] == "h" else 512
                shapes[(order, axis, kind)] = (3, *lead, MAX_ROWS[order], columns)
    return shapes


LANDINGS = landing_shapes()


def kernel(blocks_in, edge, small, out_rows, out_weights, out_vectors, *scratch):
    s = SimpleNamespace(**dict(zip(SCRATCH, scratch)))
    landing = dict(zip(LANDINGS, scratch[len(SCRATCH) :]))
    w, rows_in, h1, h2, qkv, o = s.w, s.rows_in, s.h1, s.h2, s.qkv, s.o
    r1, act, pull, probs = s.r1, s.act, s.pull, s.probs
    part, own, out_b, gr, do = s.part, s.own, s.out_b, s.gr, s.do
    tiles, norm_vec, qv_vec, up_vec = s.tiles, s.norm_vec, s.qv_vec, s.up_vec
    vec, vec_in, total = s.vec, s.vec_in, s.total

    sec = lax.axis_index(SECTION)
    y, x, core, z = (lax.axis_index(n) for n in (DP_Y, DP_X, CORE, TENSOR))
    here = {Y: y, X: x, Z: z}
    first = sec == 0

    def beside(axis, step):
        return lax.rem(here[axis] + step + SIZE[axis], SIZE[axis])

    def device(axis, step):
        return {NAME[axis]: beside(axis, step)}

    other_core = {CORE: 1 - core}
    other_section = {SECTION: 1 - sec}

    def send(src, dst, sems, where):
        return pltpu.make_async_remote_copy(
            src_ref=src, dst_ref=dst, send_sem=sems[0], recv_sem=sems[1], device_id=where, device_id_type=MESH
        )

    barrier = pltpu.get_barrier_semaphore()
    peers = [device(Y, 1), device(Y, 2), device(Y, 3), device(X, 1), other_section]
    peers += [device(Z, step) for step in (1, 2, 3)] + [other_core]
    peers += [{CORE: 1 - core, TENSOR: beside(Z, step)} for step in (1, 2, 3)]
    for peer in peers:
        pl.semaphore_signal(barrier, inc=1, device_id=peer, device_id_type=MESH)
    pl.semaphore_wait(barrier, len(peers))

    def own_rows(group):
        return w.at[group, z, y, x, pl.ds(pl.multiple_of(core * 64, 64), 64), :]

    local = [pltpu.make_async_copy(blocks_in.at[core, g], own_rows(g), s.local.at[g]) for g in range(3)]
    local.append(pltpu.make_async_copy(small, tiles.at[z, y, x, core], s.local.at[3]))
    swap = [
        send(blocks_in.at[1 - core, g], own_rows(g), (s.swap_s.at[g], s.swap_r.at[g]), other_core)
        for g in range(3)
    ]
    swap.append(send(small, tiles.at[z, y, x, core], (s.swap_s.at[3], s.swap_r.at[3]), other_core))
    for copy in swap + local:
        copy.start()

    def edge_copy(micro, half):
        to = 2 * micro + core
        src = edge.at[micro, :, pl.ds(half * 512, 512)]
        dst = rows_in.at[sec, pl.ds(pl.multiple_of(z * TILE, TILE), TILE), pl.ds(half * 512, 512)]
        stays = jnp.logical_and(to == z, core == half)
        where = {CORE: half, TENSOR: to}
        away = send(src, dst, (s.edge_s.at[micro, half], s.edge_r.at[z]), where)
        stay = pltpu.make_async_copy(src, dst, s.edge_r.at[z])
        return stays, away, stay

    def edge_start():
        for micro in range(2):
            for half in range(2):
                stays, away, stay = edge_copy(micro, half)

                @pl.when(stays)
                def _():
                    stay.start()

                @pl.when(jnp.logical_not(stays))
                def _():
                    away.start()

    half_image = rows_in.at[sec, :, pl.ds(pl.multiple_of(core * 512, 512), 512)]

    def cross():
        return send(half_image, half_image, (s.cross.at[0], s.cross.at[1]), other_core)

    def edge_arrived():
        for source in range(4):
            dst = rows_in.at[sec, pl.ds(source * TILE, TILE), pl.ds(pl.multiple_of(core * 512, 512), 512)]
            pltpu.make_async_copy(dst, dst, s.edge_r.at[source]).wait()
        cross().start()

    def edge_done():
        cross().wait()
        for micro in range(2):
            for half in range(2):
                stays, away, _ = edge_copy(micro, half)

                @pl.when(jnp.logical_not(stays))
                def _():
                    away.wait_send()

    for copy in local:
        copy.wait()
    for copy in swap:
        copy.wait()

    def region(group, at, row, rows, col, cols):
        index = [at[a] if at.get(a) is not None else slice(None) for a in (Z, Y, X)]
        return w.at[(group, *index, pl.ds(row, rows), pl.ds(col, cols))]

    def region_small(at, half):
        index = [at[a] if at.get(a) is not None else slice(None) for a in (Z, Y, X)]
        return tiles.at[(*index, slice(None) if half is None else half)]

    def gather_copy(task):
        group, order, axis, kind = task
        axes = ORDERS[order]
        done = axes[: axes.index(axis)]
        at = {a: here[a] for a in (Z, Y, X) if a not in done}
        step = -1 if kind.endswith("-") else 1
        half = None
        if kind[0] == "f":
            at[axis] = beside(axis, -step)
            half = 0 if step == 1 else 1
        sem = GATHER_TASKS[(axes, axis, kind)]
        if group == SMALL:
            ref = region_small(at, half)
            sems = (s.small_s.at[sem], s.small_r.at[sem])
        else:
            row = sum(ROWS[group][:order])
            col, cols = (0, 512) if half is None else (half * 256, 256)
            ref = region(group, at, row, ROWS[group][order], col, cols)
            sems = (s.link_s.at[group, sem], s.gather_r.at[group, sem])
        return send(ref, ref, sems, device(axis, step))

    def reduce_place(group, order, axis, at_axis, half):
        axes = ORDERS[order]
        later = axes[: axes.index(axis)]
        at = {a: here[a] for a in (Z, Y, X) if a not in later}
        at[axis] = at_axis
        row = sum(ROWS[group][:order])
        col, cols = (0, 512) if half is None else (half * 256, 256)
        return at, later, row, ROWS[group][order], col, cols

    def reduce_copy(task):
        _, group, order, axis, kind = task
        step = -1 if kind.endswith("-") else 1
        half = None
        if kind[0] == "h":
            half = 0 if step == 1 else 1
            at_axis = beside(axis, 2)
        else:
            at_axis = beside(axis, step)
        at, _, row, rows, col, cols = reduce_place(group, order, axis, at_axis, half)
        src = region(group, at, row, rows, col, cols)
        buffer = landing[(order, axis, kind)]
        lead = (slice(None),) * (len(buffer.shape) - 3)
        dst = buffer.at[(group, *lead, pl.ds(0, rows))]
        sem = REDUCE_TASKS[(ORDERS[order], axis, kind)]
        sems = (s.link_s.at[group, sem], s.reduce_r.at[group, sem])
        return send(src, dst, sems, device(axis, step))

    def part_copy(number, n):
        cols = pl.ds(n * 256 if isinstance(n, int) else pl.multiple_of(n * 256, 256), 256)
        sems = (s.part_s.at[number, n], s.part_r.at[number, n])
        return send(own.at[:, cols], part.at[number % 2, :, cols], sems, other_core)

    VEC_SLOT = {Y: 0, Z: 3, X: 6}

    def vec_copy(axis, step):
        slot = 7 if axis == CORE else VEC_SLOT[axis] + step - 1
        where = other_core if axis == CORE else device(axis, step)
        return send(vec, vec_in.at[slot], (s.vec_s.at[slot], s.vec_r.at[slot]), where)

    def copy_of(task):
        if task[0] == PART:
            return part_copy(*task[1:])
        if task[0] == VEC:
            return vec_copy(*task[1:])
        if task[0] == GRADS:
            return reduce_copy(task)
        return gather_copy(task)

    pending = []

    def emit(chains):
        links = {task for chain in chains for step in chain for task, link, _ in step.sends if link is not None}
        links -= {task for task, _, _ in EDGE_TASKS + [CROSS_TASK]}

        def run(step):
            for task in step.waits:
                if task in links:
                    copy_of(task).wait_recv()
            if step.op is not None:
                step.op()
            for task, link, _ in step.sends:
                if task in links:
                    if task[0] not in (PART, VEC):
                        pending.append(task)
                    copy_of(task).start()

        for step in in_order(chains):
            if step.where is None:
                run(step)
            else:
                pl.when(step.where)(lambda: run(step))

    def sent_all():
        for task in pending:
            copy_of(task).wait_send()
        pending.clear()

    def iota(shape, axis):
        return lax.broadcasted_iota(jnp.int32, shape, axis)

    def unpack(chunk):
        rows = tiles[chunk].reshape(256, 128)

        def spread(width, lane_of, dev_of, row_ok):
            lane = iota((128, width), 0)
            pick = (lane == lane_of(iota((128, width), 1))).astype(F32).astype(BF)
            wide = dot(rows, pick)
            i, n = iota((256, width), 0), iota((256, width), 1)
            keep = (i // 16 == dev_of(n)) & row_ok(i % 16, n)
            return jnp.where(keep, wide, 0.0).astype(BF)

        def fold(want, wide):
            a, i = iota((8, 256), 0), iota((8, 256), 1)
            return dot(want(a, i % 16).astype(F32).astype(BF), wide)

        wide = spread(
            1024,
            lambda n: n % 16,
            lambda n: jnp.where((n // 16) % 4 == chunk, n // 64, -1),
            lambda r, n: r < 6,
        )
        sums = fold(lambda a, r: a == r, wide)
        norm_vec[...] = sums if chunk == 0 else norm_vec[...] + sums
        wide = spread(
            128,
            lambda n: (2 * core + n // 64) * 4 + n % 4,
            lambda n: (n % 64) // 4,
            lambda r, n: (r == 6) | (r == 7),
        )
        both_rows = fold(lambda a, r: a == r - 6, wide)
        qv_vec[2 * chunk] = both_rows[0:1]
        qv_vec[2 * chunk + 1] = both_rows[1:2]
        wide = spread(
            512,
            lambda n: ((n // 64) % 4) * 4 + n % 4,
            lambda n: (n % 64) // 4,
            lambda r, n: r == 8 + 2 * core + n // 256,
        )
        one_row = fold(lambda a, r: (a == 0) & (r >= 0), wide)
        up_vec[2 * chunk] = one_row[0:1, :256]
        up_vec[2 * chunk + 1] = one_row[0:1, 256:]

    def vector(r):
        return norm_vec[r : r + 1, :]

    def span(i, size, align=None):
        if isinstance(i, int):
            return pl.ds(i * size, size)
        return pl.ds(pl.multiple_of(i * size, align or size), size)

    def tile(t):
        return span(t, TILE, 16)

    def both(number, rows):
        return own[rows, :].astype(F32) + part[number % 2, rows, :].astype(F32)

    def normed(value):
        centred = value - jnp.mean(value, axis=-1, keepdims=True)
        spread = jnp.mean(centred * centred, axis=-1, keepdims=True)
        scale = lax.rsqrt(spread + EPSILON)
        return centred * scale, scale

    def by_n(group, n, cut=slice(None)):
        return jnp.concatenate([w[group, g, n].reshape(256, 512)[:, cut] for g in range(4)], axis=1)

    def add_sum(row, value):
        s.sums[row] += value.reshape(value.shape[0] // 8, 8, D).sum(0)

    head_of = iota((1, 128), 1) // 64
    head_mask = [(head_of == j).astype(F32).astype(BF) for j in range(2)]

    def pick(a, b):
        return jnp.where(iota(a.shape, 1) < 64, a, b)

    def section_copy(slot, t, src):
        rows = tile(t)
        return send(src.at[rows], rows_in.at[slot, rows], (s.sec_s.at[t], s.sec_r.at[t]), other_section)

    def section_cross(slot, t):
        ref = rows_in.at[slot, tile(t)]
        return send(ref, ref, (s.sec_cross_s.at[t], s.sec_cross_r.at[t]), other_core)

    def section_pair(slot, k, use):
        mine, theirs = 2 * k + core, 2 * k + 1 - core
        section_copy(slot, mine, own).wait_recv()
        section_cross(slot, mine).start()
        use(mine)
        section_cross(slot, theirs).wait_recv()
        use(theirs)

    def section_forwarded(slot):
        for k in range(N_TILES // 2):
            section_cross(slot, 2 * k + core).wait_send()

    def section_send(slot, t, src):
        @pl.when(core == lax.rem(t, 2) if not isinstance(t, int) else core == t % 2)
        def _():
            section_copy(slot, t, src).start()

    def section_sent(slot, src):
        for k in range(N_TILES // 2):
            section_copy(slot, 2 * k + core, src).wait_send()

    def result_copy(src, owner):
        micro, owner_core = z // 2, lax.rem(z, 2)
        cols = pl.ds(pl.multiple_of(core * 512, 512), 512)
        from_ref = src.at[pl.ds(owner * TILE, TILE), cols]
        stays = jnp.logical_and(owner == z, core == owner_core)
        where = {CORE: owner_core, TENSOR: jnp.int32(owner)}
        to_ref = out_rows.at[micro, :, cols]
        sems = (s.res_s.at[owner], s.res_r.at[micro, core])
        return stays, send(from_ref, to_ref, sems, where), pltpu.make_async_copy(from_ref, to_ref, sems[1])

    def result_send(src):
        for owner in range(4):
            stays, away, stay = result_copy(src, owner)

            @pl.when(stays)
            def _():
                stay.start()

            @pl.when(jnp.logical_not(stays))
            def _():
                away.start()

    def result_sent(src):
        for owner in range(4):
            stays, away, stay = result_copy(src, owner)

            @pl.when(jnp.logical_not(stays))
            def _():
                away.wait_send()

    def norm_one(t):
        rows = tile(t)
        value, _ = normed(rows_in[0, rows, :].astype(F32))
        h1[rows, :] = (value * vector(0) + vector(1)).astype(BF)

    def project(pair):
        a, b = 2 * pair, 2 * pair + 1
        wa, wb = w[0, a].reshape(D, 512), w[0, b].reshape(D, 512)
        for half, weights in ((a, wa[:, :256]), (b, wb[:, :256])):
            p = dot(h1[...], weights)
            qkv[half, 0] = ((p[:, :128] + qv_vec[2 * half]) * 0.125).astype(BF)
            qkv[half, 1] = p[:, 128:].astype(BF)
        p = dot(h1[...], jnp.concatenate([wa[:, 256:384], wb[:, 256:384]], axis=1))
        qkv[a, 2] = (p[:, :128] + qv_vec[2 * a + 1]).astype(BF)
        qkv[b, 2] = (p[:, 128:] + qv_vec[2 * b + 1]).astype(BF)

    def attend(g):
        query, key, value = qkv[g, 0], qkv[g, 1], qkv[g, 2]
        outs = []
        for j in range(2):
            scores = dot_nt(key * head_mask[j], query)
            e = jnp.exp(scores - jnp.max(scores, axis=0, keepdims=True))
            p = (e * (1.0 / jnp.sum(e, axis=0, keepdims=True))).astype(BF)
            probs[2 * g + j] = p
            outs.append(dot_tn(p, value))
        o[:, span(g, 128)] = pick(*outs).astype(BF)

    def out_part(n):
        own[:, span(n, 256)] = dot_nt(o[...], by_n(0, n, slice(384, 512))).astype(BF)

    def norm_two(t):
        rows = tile(t)
        middle = rows_in[0, rows, :].astype(F32) + both(0, rows) + vector(2)
        r1[rows, :] = middle
        value, _ = normed(middle)
        h2[rows, :] = (value * vector(3) + vector(4)).astype(BF)

    def feed(i):
        g, half = (i // 2, i % 2) if isinstance(i, int) else (i // 2, lax.rem(i, 2))
        weights = w[1, g, :, :, :, span(half, 256)].reshape(D, 256)
        for t in range(2):
            rows = pl.ds(t * 288, 288)
            u = dot(h2[rows, :], weights) + up_vec[i]
            phi = 0.5 + 0.5 * lax.erf(u * (2.0**-0.5))
            act[rows, span(i, 256)] = (u * phi).astype(BF)
            pull[rows, span(i, 256)] = (phi + u * jnp.exp(u * u * -0.5) * 0.3989422804014327).astype(BF)

    def down(n):
        own[:, span(n, 256)] = dot_nt(act[...], by_n(2, n)).astype(BF)

    def finish(t):
        rows = tile(t)
        out_b[rows, :] = (r1[rows, :] + both(1, rows) + vector(5)).astype(BF)

    def feed_back(i):
        g, half = (i // 2, i % 2) if isinstance(i, int) else (i // 2, lax.rem(i, 2))
        ga = dot(rows_in[1], w[2, g, :, :, :, span(half, 256)].reshape(D, 256))
        du = (ga * pull[:, span(i, 256)].astype(F32)).astype(BF)
        pull[:, span(i, 256)] = du
        s.up_grad[i] = jnp.sum(du.astype(F32), axis=0, keepdims=True)

    def up_back(n):
        own[:, span(n, 256)] = dot_nt(pull[...], by_n(1, n)).astype(BF)

    def norm_back(value, grad, gain, gain_row, shift_row):
        hat, scale = normed(value)
        add_sum(gain_row, grad * hat)
        add_sum(shift_row, grad)
        dy = grad * gain
        return scale * (
            dy - jnp.mean(dy, axis=-1, keepdims=True) - hat * jnp.mean(dy * hat, axis=-1, keepdims=True)
        )

    def norm_two_back(t):
        rows = tile(t)
        pulled = norm_back(r1[rows, :], both(2, rows), vector(3), 3, 4)
        gy = rows_in[1, rows, :].astype(F32)
        grad = gy + pulled
        add_sum(5, gy)
        add_sum(2, grad)
        r1[rows, :] = grad
        gr[rows, :] = grad.astype(BF)

    def out_back(pair):
        weights = [w[0, 2 * pair + j, :, :, :, 384:512].reshape(D, 128) for j in range(2)]
        do[:, span(pair, 256)] = dot(gr[...], jnp.concatenate(weights, axis=1)).astype(BF)

    def attend_back(g):
        query, key, value = qkv[g, 0], qkv[g, 1], qkv[g, 2]
        grad = do[:, span(g, 128)]
        dq, dk, dv = [], [], []
        for j in range(2):
            p = probs[2 * g + j]
            dv.append(dot(p, grad))
            dp = dot_nt(value * head_mask[j], grad)
            p = p.astype(F32)
            ds = (p * (dp - jnp.sum(dp * p, axis=0, keepdims=True))).astype(BF)
            dk.append(dot(ds, query))
            dq.append(dot_tn(ds, key))
        dq, dk, dv = (pick(*pair).astype(BF) for pair in (dq, dk, dv))
        dq = dq * jnp.asarray(0.125, BF)
        qkv[g, 0] = dq
        qkv[g, 1] = dk
        qkv[g, 2] = dv
        s.qv_grad[2 * g] = jnp.sum(dq.astype(F32), axis=0, keepdims=True)
        s.qv_grad[2 * g + 1] = jnp.sum(dv.astype(F32), axis=0, keepdims=True)

    def qkv_all(first_g, last_g):
        return jnp.concatenate([qkv[g, k] for g in range(first_g, last_g) for k in range(3)], axis=1)

    def project_back(n):
        own[:, span(n, 256)] = dot_nt(qkv_all(0, 4), by_n(0, n, slice(0, 384))).astype(BF)

    def norm_one_back(t):
        rows = tile(t)
        pulled = norm_back(rows_in[0, rows, :].astype(F32), both(3, rows), vector(0), 0, 1)
        own[rows, :] = (r1[rows, :] + pulled).astype(BF)

    def zero_sums():
        s.sums[...] = jnp.zeros_like(s.sums)

    def fill_vec():
        vec[...] = jnp.zeros_like(vec)
        for r in range(6):
            vec[r : r + 1, :] = jnp.sum(s.sums[r], axis=0, keepdims=True)
        for r in range(8):
            vec[8 + r : 9 + r, 512:640] = s.qv_grad[r]
            vec[8 + r // 2 : 9 + r // 2, r % 2 * 256 : r % 2 * 256 + 256] = s.up_grad[r]

    def grads(group, m):
        def left(ref):
            return ref[:, m * 256 : m * 256 + 256].T

        def put(g, col, value):
            cols = value.shape[1]
            w[group, g, m, :, :, col : col + cols] = value.astype(BF).reshape(2, 128, cols)

        if group == 0:
            first_left, second_left = left(h1), left(gr)
            for pair in range(2):
                out = dot(first_left, qkv_all(2 * pair, 2 * pair + 2))
                put(2 * pair, 0, out[:, :384])
                put(2 * pair + 1, 0, out[:, 384:])
            out = dot(second_left, o[...])
            for g in range(4):
                put(g, 384, out[:, g * 128 : g * 128 + 128])
        else:
            rows, right = (h2, pull) if group == 1 else (rows_in.at[1], act)
            rows_t = left(rows)
            for g in range(4):
                put(g, 0, dot(rows_t, right[:, g * 512 : g * 512 + 512]))

    def exchanged(number):
        return [(PART, number, n) for n in range(4)]

    def part_steps(number, body, cost, waits):
        return [
            Step(waits if n == 0 else [], cost, [((PART, number, n), CORE, 295000)], partial(body, n))
            for n in range(4)
        ]

    def norm_steps(number, body, cost, after=None):
        def one(t):
            if t == 0:
                for n in range(4):
                    part_copy(number, n).wait_send()
            body(t)
            if after is not None:
                after(t)

        return [Step(exchanged(number) if t == 0 else [], cost, (), partial(one, t)) for t in range(N_TILES)]

    def everything(group):
        return [(group, order) for order in range(4)]

    forward = []
    forward += [Step([(READY, 1)] if t == 0 else [], 0.5, (), partial(norm_one, t)) for t in range(N_TILES)]
    forward += [Step(everything(0), 1.3, (), partial(project, p)) for p in range(2)]
    forward += [Step([], 1.6, (), partial(attend, g)) for g in range(4)]
    forward += part_steps(0, out_part, 0.4, [])
    forward += norm_steps(0, norm_two, 0.6)
    forward += [Step(everything(1), 0.6, (), partial(feed, i)) for i in range(8)]
    forward += part_steps(1, down, 0.8, everything(2))
    forward += norm_steps(1, finish, 0.3, lambda t: section_send(0, t, out_b))
    forward = [step._replace(where=first) for step in forward]
    unpacking = [Step([(SMALL, 0)], 1.5, (), partial(unpack, chunk)) for chunk in range(4)]
    edge_steps = [
        Step([], 0.2, EDGE_TASKS, edge_start),
        Step([(0, order) for order in range(4)], 0.2, [CROSS_TASK], edge_arrived),
        Step([CROSS_TASK[0]], 0.2, [note(READY, 1)], edge_done),
    ]
    gathers = [gather_chain(SMALL, 0)] + [gather_chain(g, o) for g in range(3) for o in range(4)]
    emit(gathers + [edge_steps, unpacking + forward])
    sent_all()

    def loop(count, body):
        def one(i, carry):
            body(i)
            return carry

        lax.fori_loop(0, count, one, 0)

    def exchange(number, body):
        def one(n):
            body(n)
            part_copy(number, n).start()

        loop(4, one)
        loop(4, lambda n: part_copy(number, n).wait())

    zero_sums()

    @pl.when(sec == 1)
    def _():
        for k in range(N_TILES // 2):
            section_pair(0, k, norm_one)
        loop(2, project)
        loop(4, attend)
        exchange(0, out_part)
        loop(4, norm_two)
        loop(8, feed)
        exchange(1, down)
        loop(4, finish)
        result_send(out_b)
        loop(8, feed_back)
        exchange(2, up_back)
        loop(4, norm_two_back)
        loop(2, out_back)
        loop(4, attend_back)
        exchange(3, project_back)

        def last(t):
            norm_one_back(t)
            section_send(1, t, own)

        loop(4, last)
        section_forwarded(0)

    def reduce_add(group, order, op):
        axis, kind = op
        if kind == "end":
            kinds = ("s",) if axis == X else ("s+", "s-")
            at_axis, half = here[axis], None
        else:
            kinds = (kind,)
            at_axis = beside(axis, 1 if kind == "h+" else -1)
            half = 0 if kind == "h+" else 1
        at, later, row, rows, col, cols = reduce_place(group, order, axis, at_axis, half)
        open_axes = [a for a in (Z, Y, X) if a in later]
        count = 1
        for a in open_axes:
            count *= SIZE[a]

        def one(i):
            rest, index = i, dict(at)
            for a in reversed(open_axes):
                index[a] = lax.rem(rest, SIZE[a])
                rest = rest // SIZE[a]
            lead = tuple(index[a] for a in open_axes)
            place = (group, index[Z], index[Y], index[X], pl.ds(row, rows), pl.ds(col, cols))
            value = w[place].astype(F32)
            for k in kinds:
                value += landing[(order, axis, k)][(group, *lead, pl.ds(0, rows), slice(None))].astype(F32)
            if later or kind != "end":
                w[place] = value.astype(BF)
            else:
                total[group, pl.ds(row, rows), :] = value

        if count == 1:
            one(0)
        else:
            loop(count, one)

    def vec_add(axis):
        value = vec[...]
        for step in range(1, SIZE[axis]):
            vec_copy(axis, step).wait_send()
            value += vec_in[VEC_SLOT[axis] + step - 1]
        vec[...] = value
        if axis == X:
            out_vectors[0] = value

    def vec_last():
        vec_copy(CORE, 1).wait_send()
        out_vectors[1] = vec_in[7]

    def vec_tasks(axis):
        return [((VEC, axis, step), VEC, 100000) for step in range(1, SIZE[axis])]

    def vec_waits(axis):
        return [(VEC, axis, step) for step in range(1, SIZE[axis])]

    vec_chain = [
        Step([(READY, 4)], 0.3, vec_tasks(Y), fill_vec),
        Step(vec_waits(Y), 0.2, vec_tasks(Z), lambda: vec_add(Y)),
        Step(vec_waits(Z), 0.2, vec_tasks(X), lambda: vec_add(Z)),
        Step(vec_waits(X), 0.2, [((VEC, CORE, 1), CORE, 65536)], lambda: vec_add(X)),
        Step([(VEC, CORE, 1)], 0.1, (), vec_last),
    ]

    def final_copy(group):
        src = total.at[group, pl.ds(pl.multiple_of((1 - core) * 64, 64), 64), :]
        return send(src, out_weights.at[group, core], (s.fin_s.at[group], s.fin_r.at[group]), other_core)

    def final_local(group):
        src = total.at[group, pl.ds(pl.multiple_of(core * 64, 64), 64), :]
        return pltpu.make_async_copy(src, out_weights.at[group, core], s.local.at[group])

    def final_start(group):
        final_copy(group).start()
        final_local(group).start()

    finals = [
        [Step([(TOTAL, group, order) for order in range(4)], 0.1, (), partial(final_start, group))]
        for group in (2, 1, 0)
    ]

    def receive_back():
        for k in range(N_TILES // 2):
            section_pair(1, k, lambda t: None)
        section_forwarded(1)

    def only_first(steps):
        return [step._replace(where=first) for step in steps]

    def grad_steps(group, cost):
        return [
            Step([], cost, [note(GRADS, group)] if m == 3 else (), partial(grads, group, m)) for m in range(4)
        ]

    backward = only_first([Step([], 0.0, (), receive_back)])
    backward += only_first([Step([], 0.35, (), partial(feed_back, i)) for i in range(8)])
    backward += grad_steps(2, 0.9)
    backward += only_first(part_steps(2, up_back, 0.8, []))
    backward += grad_steps(1, 1.0)
    backward += only_first(norm_steps(2, norm_two_back, 0.8))
    backward += only_first([Step([], 0.5, (), partial(out_back, p)) for p in range(2)])
    backward += only_first([Step([], 2.0, (), partial(attend_back, g)) for g in range(4)])
    backward += only_first(part_steps(3, project_back, 0.6, []))
    backward += grad_steps(0, 1.5)
    backward += only_first(norm_steps(3, norm_one_back, 0.8))
    backward += only_first([Step([], 0.1, (), lambda: result_send(own))])
    backward += [Step([], 0.0, [note(READY, 4)])]
    reduces = [reduce_chain(g, o, reduce_add) for g in (2, 1, 0) for o in range(4)]
    emit(reduces + finals + [vec_chain, backward])
    sent_all()

    for group in range(3):
        final_local(group).wait()
        final_copy(group).wait()

    @pl.when(first)
    def _():
        section_sent(0, out_b)
        result_sent(own)

    @pl.when(sec == 1)
    def _():
        section_sent(1, own)
        result_sent(out_b)

    for micro in range(2):
        for half in range(2):
            dst = out_rows.at[micro, :, pl.ds(half * 512, 512)]
            pltpu.make_async_copy(dst, dst, s.res_r.at[micro, half]).wait()


def dma(*shape):
    return pltpu.SemaphoreType.DMA(shape)


SCRATCH = dict(
    w=pltpu.VMEM((3, 4, 4, 2, 128, 512), BF),
    rows_in=pltpu.VMEM((2, T, D), BF),
    h1=pltpu.VMEM((T, D), BF),
    h2=pltpu.VMEM((T, D), BF),
    qkv=pltpu.VMEM((4, 3, T, 128), BF),
    o=pltpu.VMEM((T, 512), BF),
    r1=pltpu.VMEM((T, D), F32),
    act=pltpu.VMEM((T, 2048), BF),
    pull=pltpu.VMEM((T, 2048), BF),
    probs=pltpu.VMEM((8, T, T), BF),
    part=pltpu.VMEM((2, T, D), BF),
    own=pltpu.VMEM((T, D), BF),
    out_b=pltpu.VMEM((T, D), BF),
    gr=pltpu.VMEM((T, D), BF),
    do=pltpu.VMEM((T, 512), BF),
    tiles=pltpu.VMEM((4, 4, 2, 2, 16, 128), BF),
    norm_vec=pltpu.VMEM((8, D), F32),
    qv_vec=pltpu.VMEM((8, 1, 128), F32),
    up_vec=pltpu.VMEM((8, 1, 256), F32),
    sums=pltpu.VMEM((6, 8, D), F32),
    qv_grad=pltpu.VMEM((8, 1, 128), F32),
    up_grad=pltpu.VMEM((8, 1, 256), F32),
    vec=pltpu.VMEM((16, D), F32),
    vec_in=pltpu.VMEM((8, 16, D), F32),
    total=pltpu.VMEM((3, 128, 512), F32),
    local=dma(4),
    swap_s=dma(4),
    swap_r=dma(4),
    edge_s=dma(2, 2),
    edge_r=dma(4),
    cross=dma(2),
    small_s=dma(N_SMALL),
    small_r=dma(N_SMALL),
    link_s=dma(3, N_TASKS),
    gather_r=dma(3, N_TASKS),
    reduce_r=dma(3, N_TASKS),
    part_s=dma(4, N_TILES),
    part_r=dma(4, N_TILES),
    sec_s=dma(N_TILES),
    sec_r=dma(N_TILES),
    sec_cross_s=dma(N_TILES),
    sec_cross_r=dma(N_TILES),
    res_s=dma(4),
    res_r=dma(2, 2),
    vec_s=dma(8),
    vec_r=dma(8),
    fin_s=dma(3),
    fin_r=dma(3),
)


def run(blocks_in, edge, small):
    anywhere = pl.BlockSpec(memory_space=pl.ANY)
    vmem = pl.BlockSpec(memory_space=pltpu.VMEM)
    return pl.pallas_call(
        kernel,
        out_shape=(
            jax.ShapeDtypeStruct((2, TILE, D), BF),
            jax.ShapeDtypeStruct((3, 2, 64, 512), F32),
            jax.ShapeDtypeStruct((2, 16, D), F32),
        ),
        in_specs=[anywhere, anywhere, vmem],
        out_specs=(anywhere, anywhere, vmem),
        scratch_shapes=[*SCRATCH.values(), *(pltpu.VMEM(shape, BF) for shape in LANDINGS.values())],
        compiler_params=pltpu.CompilerParams(
            collective_id=0, has_side_effects=True, vmem_limit_bytes=62 << 20
        ),
    )(blocks_in, edge, small)


def body(boundary, w_qkv, qv_bias, w_out, up_weight, up_bias, down_weight, norm_bias):
    core, z = lax.axis_index(CORE), lax.axis_index(TENSOR)
    position = (lax.axis_index(DP_Y) * 2 + lax.axis_index(DP_X)) * 2 + core

    def halves(matrix):
        return jnp.moveaxis(matrix.reshape(64, 2, 512), 1, 0)

    attention = jnp.concatenate([w_qkv[0], w_out[0].T[:, None, :]], axis=1).reshape(64, 4, 2, 128)
    attention = jnp.moveaxis(attention, 2, 0).reshape(2, 64, 512)
    blocks_in = jnp.stack([attention, halves(up_weight[0]), halves(down_weight[0].T)], axis=1)
    small = jnp.concatenate([norm_bias[0], qv_bias[0].reshape(2, 16), up_bias[0].reshape(4, 16)])
    small = jnp.pad(small, ((0, 4), (0, 112)))

    out_rows, out_weights, out_vectors = run(blocks_in, boundary[0, :, 0], small)

    ends = out_rows.astype(F32)[None, :, None]
    attention = jnp.moveaxis(out_weights[0].reshape(2, 64, 4, 128), 0, 2).reshape(64, 4, 256)
    grad_up = jnp.moveaxis(out_weights[1], 0, 1).reshape(64, 1024)
    grad_down = jnp.moveaxis(out_weights[2], 0, 1).reshape(64, 1024).T
    norm_grad = lax.dynamic_slice(out_vectors[0], (0, (position * 4 + z) * 16), (6, 16))
    ordered = jnp.where(core == 0, out_vectors, out_vectors[::-1])
    qv = lax.dynamic_slice(ordered, (0, 8 + 2 * z, 512), (2, 2, 128)).reshape(2, 2, 2, 64)
    qv = jnp.moveaxis(qv, 0, 1).reshape(2, 4, 64)
    grad_qv = lax.dynamic_slice(qv, (0, 0, position * 4), (2, 4, 4))
    up = lax.dynamic_slice(ordered, (0, 8 + z, 0), (2, 1, 512)).reshape(16, 64)
    grad_up_bias = lax.dynamic_slice(up, (0, position * 4), (16, 4))
    return (
        ends,
        attention[None, :, :3],
        grad_qv[None],
        attention[:, 3].T[None],
        grad_up[None],
        grad_up_bias[None],
        grad_down[None],
        norm_grad[None],
    )


def solution(mesh):
    torus = Mesh(mesh.devices.reshape(mesh.shape[SECTION], 4, 2, 2, mesh.shape[TENSOR]), AXES)
    in_specs = (
        P(SECTION, None, DP, TENSOR, None),
        P(SECTION, DP, None, TENSOR),
        P(SECTION, None, TENSOR, DP),
        P(SECTION, TENSOR, DP),
        P(SECTION, DP, TENSOR),
        P(SECTION, TENSOR, DP),
        P(SECTION, TENSOR, DP),
        P(SECTION, None, DP_TENSOR),
    )
    return jax.shard_map(body, mesh=torus, in_specs=in_specs, out_specs=in_specs, check_vma=False)
```

time: 1280 us -> 302 us (0.24)
  waiting for transfers between devices: 328 us -> 0 us
  Pallas kernels: 0 us -> 282 us
  starting transfers between devices: 243 us -> 0 us
  blocking collectives: 215 us -> 0 us
  matrix products: 201 us -> 0 us
  other arithmetic: 143 us -> 3.69 us
  local copies, waits for them, and re-layouts: 116 us -> 10.3 us
  between operations: 17 us -> 1.04 us
    all_to_all x46 -> x0, waiting for transfers between devices: 303 us -> none  [the longest x14 200 us: sum_at_owner(): lax.all_to_all(blocks, axis, split_axis=0, concat_axis=0, tiled=True)]
    pallas_call x0 -> x1, Pallas kernels: none -> 282 us  [run(): pl.pallas_call(kernel, out_shape=(jax.ShapeDtypeStruct((2, TILE, D), BF),...]
    all_to_all x46 -> x0, starting transfers between devices: 231 us -> none  [the longest x14 75.1 us: sum_at_owner(): lax.all_to_all(blocks, axis, split_axis=0, concat_axis=0, tiled=True)]
    dot_general x57 -> x0, matrix products: 201 us -> none  [the longest x3 29.9 us: backward(): jnp.einsum('bld,fd->blf', grad_all, down_weight, preferred_element_type=j...]
    all_to_all x18 -> x0, blocking collectives: 158 us -> none  [the longest x15 95.8 us: summed_on_arrival(): lax.all_to_all(in_blocks(array, dim, peers), axis, 0, 0, tiled=True)]
    reduce_sum x90 -> x0, other arithmetic: 106 us -> none  [the longest x18 26.2 us: summed_on_arrival(): return jnp.sum(blocks.astype(jnp.float32), axis=0)]
    all_gather x3 -> x0, blocking collectives: 57.4 us -> none  [the longest x1 19.9 us: fetch_weights(): lax.all_gather(up_bias[0], DP, axis=1, tiled=True)]
    another operation x45 -> x7, local copies, waits for them, and re-layouts: 31 us -> 1.34 us  [the longest x1 0.93 us: body(): grad_up[None]]
  transfers between devices with their start and end apart: 53 -> 0, of which waited for: 38 -> 0; matrix products, arithmetic and copies ran while one was open for 28% -> 0% of each run, Pallas kernels for 0% -> 0%
where the time goes in v1:
time: 302 us; the launch traced here: 297 us
  Pallas kernels  282 us (93%)
  local copies, waits for them, and re-layouts  10.3 us (3%)
  other arithmetic  3.69 us (1%)
    pallas_call x1, Pallas kernels, run(): pl.pallas_call(kernel, out_shape=(jax.ShapeDtypeStruct((2, TILE, D), BF),...  282 us

profile of v1, /device:TPU:1, one launch (start us, length us, event | category | flops | bytes accessed | tf_op | source)
XLA Modules:
  0.0 297.2 jit_solution(17367762596613604146)
XLA Ops:
  0.7 1.0 concatenate.11
  1.6 0.1 copy.33
  1.8 0.8 concatenate.12
  2.6 0.1 maximum_bitcast_fusion
  3.0 0.8 pad_maximum_fusion.blocks_in
  3.8 0.1 copy.37
  3.9 0.1 reshape_squeeze.14
  4.0 0.6 fusion.8.small
  4.6 282.2 %shard_map.143 = (bf16[2,144,1024]{2,1,0:T(8,128)(2,1)}, f32[3,2,64,512]{3,2,1,0:T(8,128)}, f32[2,16,1024]{2,1,0:T(8,128)}) custom-call(bf16[2,3,64,512]{3,2,1,0:T(8,128)(2,1)} %pad_maximum_fusion.blocks_in, bf16[2,144,1024]{2,1,0:T(8,128)(2,1)} %bitcast.67, bf16[16,128]{1,0:T(8,128)(2,1)} %fusion.8.small), custom_call_target="tpu_custom_call" | custom-call | tf_op jit(solution)/shard_map/pallas_call | solution.py:954
  286.8 1.0 reverse_select_fusion
  287.9 0.7 dynamic-slice_bitcast_fusion
  288.8 0.7 copy.41
  289.4 0.8 slice.23
  290.4 0.6 copy.44
  290.9 1.2 slice_bitcast_fusion
  292.1 0.1 reshape_squeeze.15
  292.2 0.2 copy.38
  292.4 0.2 reshape.42
  292.7 0.7 slice_bitcast_fusion.2
  293.3 0.6 slice_bitcast_fusion.3
  294.0 0.2 copy.40
  294.2 0.9 broadcast_in_dim_reshape.3
  295.1 0.7 copy.46
  295.8 1.1 bitcast_convert_fusion
  (25 shorter events, 0.7 us)
Async XLA Ops:
  0.6 2.2 copy-start.1
  0.6 2.3 copy-start.2
  1.7 2.0 copy-start.5
  1.7 2.2 copy-start.3
  1.8 2.3 copy-start.4
  292.6 3.2 %copy-start = (bf16[2,144,1024]{2,1,0:T(8,128)(2,1)S(1)}, bf16[2,144,1024]{2,1,0:T(8,128)(2,1)}, u32[]{:S(2)}) copy-start(bf16[2,144,1024]{2,1,0:T(8,128)(2,1)} %get-tuple-element.11) | copy-start | bytes 1769476
